TPU v7x, 128 devices: a whole 4x4x4 slice. The times are simulated.
128 devices in a mesh: dp: 16 (over y, x_hi, core), tensor: 8 (over z, x_lo).
Axes of the slice: x: 4 (x_hi: 2, x_lo: 2; x = x_hi * 2 + x_lo), y: 4, z: 4, core: 2. Of those that a mesh axis runs over, the one named last changes fastest.
Arguments:
- tokens: bfloat16 [8192, 4096], P(('dp', 'tensor')), may hold values from -24 to 24
- w_up: bfloat16 [4096, 8192], P(None, 'tensor'), may hold values from -0.125 to 0.125
- w_down: bfloat16 [8192, 4096], P('tensor'), may hold values from -0.09375 to 0.09375
- mask_up: int32 [64, 128], P(None, 'tensor'), may hold values from 0 to 1, as said below
- mask_down: int32 [128, 64], P('tensor'), may hold values from 0 to 1, as said below
- cotangent: bfloat16 [8192, 4096], P(('dp', 'tensor')), may hold values from -24 to 24
Outputs:
- output: bfloat16 [8192, 4096], P(('dp', 'tensor'))
- grad_tokens: bfloat16 [8192, 4096], P(('dp', 'tensor'))
- grad_up: float32 [4096, 8192], P('dp', 'tensor')
- grad_down: float32 [8192, 4096], P('tensor', 'dp')
Inputs may be any that keep to these rules, and one draw needn't show every extreme that they name: `mask_up`: split into aligned groups of 4 block rows by 16 block columns, every group keeps at most 40 blocks, and some group keeps exactly 40. `mask_down`: split into aligned groups of 16 block rows by 4 block columns, every group keeps at most 40 blocks, and some group keeps exactly 40.
All inputs are finite; a program needn't handle non-finite values.
Results may differ from a plain program's by a relative error of at most 0.019.
Values may be sent and summed in bfloat16 or wider, within the bound.
No kernel may reach another device: no remote copies, remote signals or barrier semaphores. Data moves between devices by JAX's collectives and lax.ppermute only.
A program may use at most 256 MiB of HBM per device.

v0:
```python
import math

import jax
import jax.numpy as jnp
from jax import lax
from jax.sharding import PartitionSpec as P

B = 64


def gelu_tanh(value):
    inner = math.sqrt(2.0 / math.pi) * (value + 0.044715 * value * value * value)
    return 0.5 * value * (1.0 + jnp.tanh(inner))


def gelu_slope(value):
    coeff = math.sqrt(2.0 / math.pi)
    tanh_part = jnp.tanh(coeff * (value + 0.044715 * value * value * value))
    return 0.5 * (1.0 + tanh_part) + 0.5 * value * (1.0 - tanh_part * tanh_part) * coeff * (
        1.0 + 3.0 * 0.044715 * value * value
    )


def apply_mask(weight, mask):
    nrows, ncols = mask.shape
    shaped = weight.reshape(nrows, B, ncols, B) * mask.astype(weight.dtype)[:, None, :, None]
    return shaped.reshape(weight.shape)


def local(tokens, w_up, w_down, mask_up, mask_down, cotangent):
    rows_x, rows_dy = (
        lax.all_gather(tokens, "tensor", axis=0, tiled=True),
        lax.all_gather(cotangent, "tensor", axis=0, tiled=True),
    )
    up_kept = apply_mask(w_up, mask_up)
    down_kept = apply_mask(w_down, mask_down)
    pre = jnp.dot(rows_x, up_kept, preferred_element_type=jnp.float32)
    hidden = gelu_tanh(pre).astype(jnp.bfloat16)
    piece = hidden
    output = lax.psum_scatter(
        jnp.dot(piece, down_kept, preferred_element_type=jnp.float32).astype(jnp.bfloat16),
        "tensor",
        scatter_dimension=0,
        tiled=True,
    )
    local_down = lax.dot_general(
        hidden, rows_dy, (((0,), (0,)), ((), ())), preferred_element_type=jnp.float32
    )
    local_down = apply_mask(local_down, mask_down)
    grad_down = lax.psum_scatter(
        local_down.astype(jnp.bfloat16), "dp", scatter_dimension=1, tiled=True
    ).astype(jnp.float32)
    grad_hidden = lax.dot_general(
        rows_dy, down_kept, (((1,), (1,)), ((), ())), preferred_element_type=jnp.float32
    )
    grad_pre = (grad_hidden * gelu_slope(pre)).astype(jnp.bfloat16)
    piece = grad_pre
    grad_tokens = lax.psum_scatter(
        lax.dot_general(
            piece, up_kept, (((1,), (1,)), ((), ())), preferred_element_type=jnp.float32
        ).astype(jnp.bfloat16),
        "tensor",
        scatter_dimension=0,
        tiled=True,
    )
    local_up = lax.dot_general(
        rows_x, grad_pre, (((0,), (0,)), ((), ())), preferred_element_type=jnp.float32
    )
    local_up = apply_mask(local_up, mask_up)
    grad_up = lax.psum_scatter(
        local_up.astype(jnp.bfloat16), "dp", scatter_dimension=0, tiled=True
    ).astype(jnp.float32)
    return (output, grad_tokens, grad_up, grad_down)


def solution(mesh):
    placed = (
        P(("dp", "tensor"), None),
        P(None, "tensor"),
        P("tensor", None),
        P(None, "tensor"),
        P("tensor", None),
        P(("dp", "tensor"), None),
    )
    return jax.shard_map(
        local,
        mesh=mesh,
        in_specs=placed,
        out_specs=(
            P(("dp", "tensor"), None),
            P(("dp", "tensor"), None),
            P("dp", "tensor"),
            P("tensor", "dp"),
        ),
        check_vma=False,
    )
```

profile of v0, /device:TPU:24, one launch (start us, length us, event | category | flops | bytes accessed | tf_op | source)
XLA Modules:
  0.0 608.4 jit_solution(7236030214603168126)
XLA Ops:
  7.2 0.7 all-gather.3.cloned.1.call-update
  7.9 0.7 all-gather.5.cloned.1.call-update
  8.7 0.8 fusion.17
  9.6 6.1 %mul.94 = bf16[64,64,16,64]{3,2,1,0:T(8,128)(2,1)} broadcast(bf16[64,16]{1,0:T(8,128)(2,1)S(1)} %copy.10), dimensions={0,2} | broadcast | bytes 8390656 | tf_op jit(solution)/shard_map/mul | solution.py:26
  15.7 22.7 %mul.95 = bf16[4096,1024]{1,0:T(8,128)(2,1)} reshape(bf16[64,64,16,64]{3,2,1,0:T(8,128)(2,1)} %mul.94) | data formatting | bytes 16777216 | tf_op jit(solution)/shard_map/mul | solution.py:26
  38.4 11.4 %mul.118 = f32[16,64,64,64]{3,2,1,0:T(8,128)} broadcast(f32[16,64]{1,0:T(8,128)S(1)} %get-tuple-element.8), dimensions={0,2} | broadcast | bytes 16781312 | tf_op jit(solution)/shard_map/mul | solution.py:26
  49.8 28.0 %mul.119 = f32[1024,4096]{1,0:T(8,128)} reshape(f32[16,64,64,64]{3,2,1,0:T(8,128)} %mul.118) | data formatting | bytes 33554432 | tf_op jit(solution)/shard_map/mul | solution.py:26
  77.8 25.0 %all-gather.3.cloned.1.call-done = bf16[512,4096]{1,0:T(8,128)(2,1)} async-done(((bf16[64,4096]{1,0:T(8,128)(2,1)}), bf16[512,4096]{1,0:T(8,128)(2,1)}) %all-gather.3.cloned.1.call-update) | async-done | bytes 4194320 | tf_op jit(solution)/shard_map/all_gather | solution.py:32
  102.7 9.5 %fusion.5 = f32[1024,512]{1,0:T(8,128)S(1)} fusion(bf16[512,4096]{1,0:T(8,128)(2,1)} %all-gather.3.cloned.1.call-done, bf16[4096,1024]{1,0:T(8,128)(2,1)} %param.7, bf16[4096,1024]{1,0:T(8,128)(2,1)} %mul.95), kind=kOutput, calls=%fused_computation.9 | convolution fusion | flops 4299161600 | bytes 23068672 | tf_op jit(solution)/shard_map/dot_general | solution.py:37
  112.2 82.9 %all-gather.5.cloned.1.call-done = bf16[512,4096]{1,0:T(8,128)(2,1)} async-done(((bf16[64,4096]{1,0:T(8,128)(2,1)}), bf16[512,4096]{1,0:T(8,128)(2,1)}) %all-gather.5.cloned.1.call-update) | async-done | bytes 4194320 | tf_op jit(solution)/shard_map/all_gather | solution.py:33
  195.2 11.4 %multiply_convert_fusion = bf16[1024,4096]{1,0:T(8,128)(2,1)} fusion(f32[1024,4096]{1,0:T(8,128)} %mul.119, bf16[512,4096]{1,0:T(8,128)(2,1)} %all-gather.5.cloned.1.call-done, f32[1024,512]{1,0:T(8,128)S(1)} %fusion.5), kind=kOutput, calls=%fused_computation.2 | convolution fusion | flops 4308074496 | bytes 31457280 | tf_op jit(solution)/shard_map/dot_general | solution.py:46
  206.9 6.5 %mul.103 = bf16[16,64,64,64]{3,2,1,0:T(8,128)(2,1)} broadcast(bf16[16,64]{1,0:T(8,128)(2,1)S(1)} %get-tuple-element.9), dimensions={0,2} | broadcast | bytes 8390656 | tf_op jit(solution)/shard_map/mul | solution.py:26
  213.4 23.3 %mul.104 = bf16[1024,4096]{1,0:T(8,128)(2,1)} reshape(bf16[16,64,64,64]{3,2,1,0:T(8,128)(2,1)} %mul.103) | data formatting | bytes 16777216 | tf_op jit(solution)/shard_map/mul | solution.py:26
  236.6 11.6 %mul.115 = f32[64,64,16,64]{1,0,3,2:T(8,128)} broadcast(f32[64,16]{0,1:T(8,128)S(1)} %get-tuple-element.10), dimensions={0,2} | broadcast | bytes 16781312 | tf_op jit(solution)/shard_map/mul | solution.py:26
  248.2 28.2 %mul.116 = f32[4096,1024]{0,1:T(8,128)} reshape(f32[64,64,16,64]{1,0,3,2:T(8,128)} %mul.115) | data formatting | bytes 33554432 | tf_op jit(solution)/shard_map/mul | solution.py:26
  276.3 12.8 %fusion.13 = bf16[512,1024]{0,1:T(8,128)(2,1)S(1)} fusion(f32[1024,512]{1,0:T(8,128)S(1)} %fusion.5, bf16[512,4096]{1,0:T(8,128)(2,1)} %all-gather.5.cloned.1.call-done, bf16[1024,4096]{1,0:T(8,128)(2,1)} %param.8, bf16[1024,4096]{1,0:T(8,128)(2,1)} %mul.104), kind=kOutput, calls=%fused_computation.19 | convolution fusion | flops 4309123072 | bytes 24117248 | tf_op jit(solution)/shard_map/dot_general | solution.py:53
  289.2 10.6 %fusion = bf16[4096,1024]{0,1:T(8,128)(2,1)} fusion(f32[4096,1024]{0,1:T(8,128)} %mul.116, bf16[512,1024]{0,1:T(8,128)(2,1)S(1)} %fusion.13, bf16[512,4096]{1,0:T(8,128)(2,1)S(1)} %copy-done), kind=kOutput, calls=%fused_computation.1 | convolution fusion | flops 4303355904 | bytes 30408704 | tf_op jit(solution)/shard_map/dot_general | solution.py:66
  299.9 12.9 %convolution_convert_fusion = bf16[512,4096]{1,0:T(8,128)(2,1)} fusion(bf16[512,1024]{0,1:T(8,128)(2,1)S(1)} %fusion.13, bf16[4096,1024]{1,0:T(8,128)(2,1)} %param.7, bf16[4096,1024]{1,0:T(8,128)(2,1)} %mul.95), kind=kOutput, calls=%fused_computation.3 | convolution fusion | flops 4301258752 | bytes 22020096 | tf_op jit(solution)/shard_map/dot_general | solution.py:59
  313.0 12.4 %convolution_convert_fusion.1 = bf16[512,4096]{1,0:T(8,128)(2,1)} fusion(bf16[1024,4096]{1,0:T(8,128)(2,1)} %param.8, bf16[1024,4096]{1,0:T(8,128)(2,1)} %mul.104, f32[1024,512]{1,0:T(8,128)S(1)} %fusion.5), kind=kOutput, calls=%fused_computation.4 | convolution fusion | flops 4305977344 | bytes 23068672 | tf_op jit(solution)/shard_map/dot_general | solution.py:41
  325.5 2.2 convert_element_type.47
  327.7 86.4 %reduce-scatter.9.cloned.1.call-done = bf16[256,1024]{0,1:T(8,128)(2,1)} async-done(((bf16[4096,1024]{0,1:T(8,128)(2,1)}), bf16[256,1024]{0,1:T(8,128)(2,1)}) %reduce-scatter.9.cloned.1.call-update) | async-done | bytes 524304 | tf_op jit(solution)/shard_map/reduce_scatter | solution.py:70
  414.1 2.2 copy.11
  416.3 91.2 %reduce-scatter.7.cloned.1.call-done = bf16[64,4096]{1,0:T(8,128)(2,1)} async-done(((bf16[512,4096]{1,0:T(8,128)(2,1)}), bf16[64,4096]{1,0:T(8,128)(2,1)}) %reduce-scatter.7.cloned.1.call-update) | async-done | bytes 524304 | tf_op jit(solution)/shard_map/reduce_scatter | solution.py:58
  507.5 94.1 %reduce-scatter.5.cloned.1.call-done = bf16[64,4096]{1,0:T(8,128)(2,1)} async-done(((bf16[512,4096]{1,0:T(8,128)(2,1)}), bf16[64,4096]{1,0:T(8,128)(2,1)}) %reduce-scatter.5.cloned.1.call-update) | async-done | bytes 524304 | tf_op jit(solution)/shard_map/reduce_scatter | solution.py:40
  (17 shorter events, 0.8 us)
Async XLA Ops:
  7.2 95.6 %all-gather.3.cloned.1.call-start = ((), (), s32[]{:S(2)}) async-start(), calls=%async_computation.4 | async-start | bytes 4718592 | tf_op jit(solution)/shard_map/all_gather | solution.py:32
  7.9 187.3 %all-gather.5.cloned.1.call-start = ((), (), s32[]{:S(2)}) async-start(), calls=%async_computation.6 | async-start | bytes 4718592 | tf_op jit(solution)/shard_map/all_gather | solution.py:33
  8.6 316.8 %reduce-scatter.11.cloned.1.call-start = ((), (), s32[]{:S(2)}) async-start(), calls=%async_computation.9 | async-start | bytes 8912896 | tf_op jit(solution)/shard_map/reduce_scatter | solution.py:50
  15.7 22.7 %copy-start.1 = (s32[16,64]{1,0:T(8,128)S(1)}, s32[16,64]{1,0:T(8,128)}, u32[]{:S(2)}) copy-start(s32[16,64]{1,0:T(8,128)} %param.10) | copy-start | bytes 12292
  206.6 207.4 %reduce-scatter.9.cloned.1.call-start = ((), (), s32[]{:S(2)}) async-start(), calls=%async_computation.8 | async-start | bytes 8912896 | tf_op jit(solution)/shard_map/reduce_scatter | solution.py:70
  276.3 12.8 %copy-start = (bf16[512,4096]{1,0:T(8,128)(2,1)S(1)}, bf16[512,4096]{1,0:T(8,128)(2,1)}, u32[]{:S(2)}) copy-start(bf16[512,4096]{1,0:T(8,128)(2,1)} %all-gather.3.cloned.1.call-done) | copy-start | bytes 12582916
  299.8 207.7 %reduce-scatter.7.cloned.1.call-start = ((), (), s32[]{:S(2)}) async-start(), calls=%async_computation.7 | async-start | bytes 4718592 | tf_op jit(solution)/shard_map/reduce_scatter | solution.py:58
  312.7 288.9 %reduce-scatter.5.cloned.1.call-start = ((), (), s32[]{:S(2)}) async-start(), calls=%async_computation.5 | async-start | bytes 4718592 | tf_op jit(solution)/shard_map/reduce_scatter | solution.py:40
Sparse Core Ops, SparseCore 0:
  9.6 93.0 all-gather.2
  104.4 90.7 all-gather.4
  206.8 101.9 reduce-scatter.10
  312.8 101.1 reduce-scatter.8
  416.9 90.5 reduce-scatter.6
  510.3 91.2 reduce-scatter.4
where the time goes:
time: 611 us; the launch traced here: 608 us
  waiting for transfers between devices  381 us (62%)
  local copies, waits for them, and re-layouts  140 us (23%)
  matrix products  69.7 us (11%)
  between operations  14.1 us (2%)
    mul x8, local copies, waits for them, and re-layouts, apply_mask(): weight.reshape(nrows, B, ncols, B)  138 us
    reduce_scatter x1, waiting for transfers between devices, local(): lax.psum_scatter(jnp.dot(piece, down_kept, preferred_element_type=jnp.flo...  94.1 us
    reduce_scatter x1, waiting for transfers between devices, local(): lax.psum_scatter(lax.dot_general(piece, up_kept, (((1,), (1,)), ((), ()))...  91.2 us
    reduce_scatter x1, waiting for transfers between devices, local(): lax.psum_scatter(local_up.astype(jnp.bfloat16), 'dp', scatter_dimension=0...  86.4 us
    all_gather x1, waiting for transfers between devices, local(): lax.all_gather(cotangent, 'tensor', axis=0, tiled=True)  82.9 us
    all_gather x1, waiting for transfers between devices, local(): lax.all_gather(tokens, 'tensor', axis=0, tiled=True)  25 us
    dot_general x1, matrix products, local(): lax.dot_general(piece, up_kept, (((1,), (1,)), ((), ())), preferred_eleme...  12.9 us
    dot_general x1, matrix products, local(): lax.dot_general(rows_dy, down_kept, (((1,), (1,)), ((), ())), preferred_e...  12.8 us
  transfers between devices with their start and end apart: 6, of which 5 were waited for; matrix products, arithmetic and copies ran while one was open for 33% of the time, Pallas kernels for 0%

commit v1 on v0

v1 whole, which is shorter than its diff:
```python
import functools
import math

import jax
import jax.numpy as jnp
from jax import lax
from jax.experimental import pallas as pl
from jax.experimental.pallas import tpu as pltpu
from jax.sharding import PartitionSpec as P

B = 64
D = 4096
F = 1024
KEPT = 40
SLAB = KEPT // 2 * B
MIB = 1 << 20
C = math.sqrt(2.0 / math.pi)
f32, bf16 = jnp.float32, jnp.bfloat16
AXES = ("dp", "tensor")


def device_at(x, y, z, c):
    x, y, z = x % 4, y % 4, z % 4
    return ((y * 2 + x // 2) * 2 + c) * 8 + z * 2 + x % 2


def shift(value, dx=0, dy=0, dz=0, dc=0):
    pairs = [
        (device_at(x, y, z, c), device_at(x + dx, y + dy, z + dz, c ^ dc))
        for x in range(4)
        for y in range(4)
        for z in range(4)
        for c in range(2)
    ]
    return lax.ppermute(value, AXES, pairs)


def cost(flops, nbytes):
    return pl.CostEstimate(flops=int(flops), bytes_accessed=int(nbytes), transcendentals=0)


def spread(blocks):
    row = lax.broadcasted_iota(jnp.int32, (blocks, blocks * B), 0)
    col = lax.broadcasted_iota(jnp.int32, (blocks, blocks * B), 1)
    return (row == col // B).astype(f32).astype(bf16)


def mask_kernel(mu, md, wu, wd, uk, dk, su, sd):
    i = pl.program_id(0)

    @pl.when(i == 0)
    def _():
        su[...] = jnp.dot(mu[...].astype(f32).astype(bf16), spread(16), preferred_element_type=f32)
        sd[...] = jnp.dot(md[...].astype(f32).astype(bf16), spread(64), preferred_element_type=f32)

    for k in range(4):
        row = su[pl.ds(4 * i + k, 1), :]
        block = wu[k * B : (k + 1) * B, :]
        uk[k * B : (k + 1) * B, :] = (block.astype(f32) * row).astype(bf16)
    dk[...] = (wd[...].astype(f32) * sd[pl.ds(i, 1), :]).astype(bf16)


def kept_weights(w_up, w_down, mask_up, mask_down):
    return pl.pallas_call(
        mask_kernel,
        grid=(16,),
        in_specs=[
            pl.BlockSpec((64, 16), lambda i: (0, 0)),
            pl.BlockSpec((16, 64), lambda i: (0, 0)),
            pl.BlockSpec((256, F), lambda i: (i, 0)),
            pl.BlockSpec((64, D), lambda i: (i, 0)),
        ],
        out_specs=[
            pl.BlockSpec((256, F), lambda i: (i, 0)),
            pl.BlockSpec((64, D), lambda i: (i, 0)),
        ],
        out_shape=[jax.ShapeDtypeStruct((D, F), bf16), jax.ShapeDtypeStruct((F, D), bf16)],
        scratch_shapes=[pltpu.VMEM((64, F), f32), pltpu.VMEM((16, D), f32)],
        compiler_params=pltpu.CompilerParams(vmem_limit_bytes=24 * MIB),
        cost_estimate=cost(0, 36 * MIB),
        name="kept_weights",
    )(mask_up, mask_down, w_up, w_down)


def front_kernel(copies, n_pieces, *refs):
    pieces = refs[:n_pieces]
    uk, dk, hid, gp, hid_t, gp_t, xf, df, sem = refs[n_pieces:]

    @pl.when(pl.program_id(0) == 0)
    def _():
        moves = [
            pltpu.make_async_copy(
                pieces[p].at[pl.ds(src, n), :], (xf, df)[to].at[pl.ds(dst, n), :], sem.at[k]
            )
            for k, (p, src, n, to, dst) in enumerate(copies)
        ]
        for move in moves:
            move.start()
        for move in moves:
            move.wait()

    pre = jnp.dot(xf[...], uk[...], preferred_element_type=f32)
    back = lax.dot_general(df[...], dk[...], (((1,), (1,)), ((), ())), preferred_element_type=f32)
    t = jnp.tanh(C * (pre + 0.044715 * pre * pre * pre))
    h = 0.5 * pre * (1.0 + t)
    slope = 0.5 * (1.0 + t) + 0.5 * pre * (1.0 - t * t) * C * (1.0 + 3.0 * 0.044715 * pre * pre)
    g = back * slope
    hid[...] = h.astype(bf16)
    gp[...] = g.astype(bf16)
    hid_t[...] = h.T.astype(bf16)
    gp_t[...] = g.T.astype(bf16)


def front(pieces, copies, up_kept, down_kept):
    n, tile = len(pieces), 256
    any_spec = pl.BlockSpec(memory_space=pl.ANY)
    whole = pl.BlockSpec((256, D), lambda i: (0, 0))
    across = pl.BlockSpec((256, tile), lambda i: (0, i))
    down = pl.BlockSpec((tile, 256), lambda i: (i, 0))
    return pl.pallas_call(
        functools.partial(front_kernel, copies, n),
        grid=(F // tile,),
        in_specs=[any_spec] * n
        + [pl.BlockSpec((D, tile), lambda i: (0, i)), pl.BlockSpec((tile, D), lambda i: (i, 0))],
        out_specs=[across, across, down, down, whole, whole],
        out_shape=[
            jax.ShapeDtypeStruct((256, F), bf16),
            jax.ShapeDtypeStruct((256, F), bf16),
            jax.ShapeDtypeStruct((F, 256), bf16),
            jax.ShapeDtypeStruct((F, 256), bf16),
            jax.ShapeDtypeStruct((256, D), bf16),
            jax.ShapeDtypeStruct((256, D), bf16),
        ],
        scratch_shapes=[pltpu.SemaphoreType.DMA((len(copies),))],
        compiler_params=pltpu.CompilerParams(vmem_limit_bytes=40 * MIB),
        cost_estimate=cost(4 * 256 * D * F, 26 * MIB),
        name="front",
    )(*pieces, up_kept, down_kept)


COLUMN = (
    (0, 0, 64, 0, 0),
    (1, 0, 64, 0, 64),
    (2, 0, 64, 0, 128),
    (6, 0, 32, 0, 192),
    (7, 0, 32, 0, 224),
    (3, 0, 64, 1, 0),
    (4, 0, 64, 1, 64),
    (5, 0, 64, 1, 128),
    (6, 32, 32, 1, 192),
    (7, 32, 32, 1, 224),
)
SIDE = tuple(
    (p + 4 * s, src, n, to, dst + 128 * s)
    for s in range(2)
    for p, src, n, to, dst in (
        (0, 0, 32, 0, 0),
        (1, 0, 64, 0, 32),
        (3, 0, 32, 0, 96),
        (0, 32, 32, 1, 0),
        (2, 0, 64, 1, 32),
        (3, 32, 32, 1, 96),
    )
)


def shares(hid, gp, uk, dk):
    o = jnp.dot(hid[...], dk[...], preferred_element_type=f32).astype(bf16)
    t = lax.dot_general(
        gp[...], uk[...], (((1,), (1,)), ((), ())), preferred_element_type=f32
    ).astype(bf16)
    return o, t


def column_kernel(hid, gp, uk, dk, o_ref, t_ref):
    o_ref[...], t_ref[...] = shares(hid, gp, uk, dk)


def side_kernel(hid, gp, uk, dk, *outs):
    o, t = shares(hid, gp, uk, dk)
    for s in range(2):
        q1, q2, q3, q4 = outs[4 * s : 4 * s + 4]
        a = 128 * s
        q1[0:32, :], q1[32:64, :] = o[a + 96 : a + 128, :], t[a + 96 : a + 128, :]
        q2[...] = o[a + 32 : a + 96, :]
        q3[...] = t[a + 32 : a + 96, :]
        q4[0:32, :], q4[32:64, :] = o[a : a + 32, :], t[a : a + 32, :]


def back_shares(kernel, n_out, rows, hid, gp, up_kept, down_kept):
    tile = 512
    return pl.pallas_call(
        kernel,
        grid=(D // tile,),
        in_specs=[
            pl.BlockSpec((256, F), lambda i: (0, 0)),
            pl.BlockSpec((256, F), lambda i: (0, 0)),
            pl.BlockSpec((tile, F), lambda i: (i, 0)),
            pl.BlockSpec((F, tile), lambda i: (0, i)),
        ],
        out_specs=[pl.BlockSpec((rows, tile), lambda i: (0, i))] * n_out,
        out_shape=[jax.ShapeDtypeStruct((rows, D), bf16)] * n_out,
        compiler_params=pltpu.CompilerParams(vmem_limit_bytes=24 * MIB),
        cost_estimate=cost(4 * 256 * D * F, 22 * MIB),
        name="shares",
    )(hid, gp, up_kept, down_kept)


def packed_kernel(groups, blocks, a1, a2, b1, b2, out, t):
    j = groups[pl.program_id(0)]
    for r in range(0, F, 256):
        rows = slice(r, r + 256)
        acc = jnp.dot(a1[rows, :], b1[...], preferred_element_type=f32)
        acc += jnp.dot(a2[rows, :], b2[...], preferred_element_type=f32)
        for ct in range(2):
            part = acc[:, ct * 128 : (ct + 1) * 128]
            t[ct, rows, :] = part.astype(bf16)
            t[2 + ct, rows, :] = pltpu.roll(part, 64, 1).astype(bf16)
    for p in range(KEPT // 2):
        ia, ib = blocks[j, 2 * p], blocks[j, 2 * p + 1]
        ra = pl.multiple_of((ia // 4) * B, B)
        rb = pl.multiple_of((ib // 4) * B, B)
        va = (ia % 2) * 2 + (ia % 4) // 2
        vb = (1 - ib % 2) * 2 + (ib % 4) // 2
        to = slice(p * B, (p + 1) * B)
        out[0, to, 0:B] = t[va, pl.ds(ra, B), 0:B]
        out[0, to, B : 2 * B] = t[vb, pl.ds(rb, B), B : 2 * B]


def packed(groups, blocks, a1, a2, b1, b2):
    left = pl.BlockSpec((F, 256), lambda j, g, k: (0, 0))
    right = pl.BlockSpec((256, 256), lambda j, g, k: (0, g[j]))
    return pl.pallas_call(
        packed_kernel,
        grid_spec=pltpu.PrefetchScalarGridSpec(
            num_scalar_prefetch=2,
            grid=(8,),
            in_specs=[left, left, right, right],
            out_specs=pl.BlockSpec((1, SLAB, 128), lambda j, g, k: (j, 0, 0)),
            scratch_shapes=[pltpu.VMEM((4, F, 128), bf16)],
        ),
        out_shape=jax.ShapeDtypeStruct((8, SLAB, 128), bf16),
        compiler_params=pltpu.CompilerParams(vmem_limit_bytes=24 * MIB),
        cost_estimate=cost(2 * 512 * F * 2048, 6 * MIB),
        name="packed",
    )(groups, blocks, a1, a2, b1, b2)


def expand_kernel(turned, places, w, f, out, s, dense):
    total = w[0].astype(f32) + f[0].astype(f32)
    s[0] = total
    s[1] = pltpu.roll(total, 64, 1)
    target = dense if turned else out
    for r in range(16):
        rows = slice(r * B, (r + 1) * B)
        for c in range(4):
            slot = places[r * 4 + c]
            at = jnp.maximum(slot, 0)
            row = pl.multiple_of((at // 2) * B, B)
            half = slice((c % 2) * B, (c % 2 + 1) * B)
            version = at % 2 if c % 2 == 0 else 1 - at % 2
            block = s[version, pl.ds(row, B), half]
            target[rows, c * B : (c + 1) * B] = jnp.where(slot >= 0, block, 0.0)
    if turned:
        for r in range(0, F, 128):
            for c in range(0, 256, 128):
                out[c : c + 128, r : r + 128] = dense[r : r + 128, c : c + 128].T


def expand(turned, places, w, f):
    slab = pl.BlockSpec((1, SLAB, 128), lambda i, p: (0, 0, 0))
    shape = (256, F) if turned else (F, 256)
    return pl.pallas_call(
        functools.partial(expand_kernel, turned),
        grid_spec=pltpu.PrefetchScalarGridSpec(
            num_scalar_prefetch=1,
            grid=(1,),
            in_specs=[slab, slab],
            out_specs=pl.BlockSpec(shape, lambda i, p: (0, 0)),
            scratch_shapes=[pltpu.VMEM((2, SLAB, 128), f32), pltpu.VMEM((F, 256), f32)],
        ),
        out_shape=jax.ShapeDtypeStruct(shape, f32),
        compiler_params=pltpu.CompilerParams(vmem_limit_bytes=24 * MIB),
        cost_estimate=cost(0, 2 * MIB),
        name="expand",
    )(places, w, f)


def plan(mask_up, mask_down):
    up = mask_up.reshape(16, 4, 16).transpose(0, 2, 1).reshape(16, 64)
    down = mask_down.reshape(16, 16, 4).transpose(1, 0, 2).reshape(16, 64)
    keep = (jnp.stack([up, down]) != 0).astype(jnp.int32)
    place = jnp.arange(64, dtype=jnp.int32)
    slot = jnp.sum(keep[:, :, None, :] * (place[None, :] < place[:, None]), axis=-1)
    wanted = jnp.arange(KEPT, dtype=jnp.int32)
    hit = (slot[:, :, None, :] == wanted[:, None]) & (keep[:, :, None, :] != 0)
    blocks = jnp.sum(jnp.where(hit, place, 0), axis=-1)
    places = jnp.where(keep != 0, slot, -1)
    return blocks, places


def add(*terms):
    total = terms[0].astype(f32)
    for term in terms[1:]:
        total = total + term.astype(f32)
    return total.astype(bf16)


def cat(*parts):
    return jnp.concatenate(parts, axis=0)


def dp_sum(mine, theirs):
    got = shift(theirs, dc=1)
    v = [add(mine[k : k + 1], got[k : k + 1]) for k in (0, 1)]
    low, high = shift(v[0], dy=1), shift(v[1], dy=-1)
    ahead = cat(add(mine[2:3], got[2:3], low), add(mine[3:4], got[3:4]))
    behind = cat(add(mine[4:5], got[4:5]), add(mine[5:6], got[5:6], high))
    from_behind, from_ahead = shift(ahead, dy=1), shift(behind, dy=-1)
    far = add(mine[7:8], got[7:8], from_behind[1:2], from_ahead[1:2])
    near = add(mine[6:7], got[6:7], from_behind[0:1], from_ahead[0:1])
    return near, shift(far, dx=2)


def local(tokens, w_up, w_down, mask_up, mask_down, cotangent):
    x, d = tokens, cotangent
    dp = lax.axis_index("dp")
    y, xh, c = dp // 4, (dp // 2) % 2, dp % 2

    xm, xp = shift(x, dz=1), shift(x, dz=-1)
    l1, r1 = shift(cat(x[:32], d[:32]), dx=1), shift(cat(x[32:], d[32:]), dx=-1)
    dm, dp_ = shift(d, dz=1), shift(d, dz=-1)
    l2 = shift(cat(xm[:32], xp[:32]), dx=1)
    r2 = shift(cat(xm[32:], xp[32:]), dx=-1)
    two_a = shift(cat(xm[:32], dm[:32]), dz=1)
    two_b = shift(cat(xp[32:], dp_[32:]), dz=-1)
    l3 = shift(cat(dm[:32], dp_[:32]), dx=1)
    r3 = shift(cat(dm[32:], dp_[32:]), dx=-1)
    l4, r4 = shift(two_a, dx=1), shift(two_b, dx=-1)

    uk, dk = kept_weights(w_up, w_down, mask_up, mask_down)
    blocks, places = plan(mask_up, mask_down)
    order = [(2, 0), (2, 1), (1, 0), (1, 1), (3, 0), (3, 1), (0, 0), (0, 1)]
    near = jnp.stack([((y + dy) % 4) * 4 + (xh ^ e) * 2 + c for dy, e in order]).astype(jnp.int32)
    away = near ^ 1
    own = lax.dynamic_index_in_dim(places, dp, 1, keepdims=False)

    hid1, gp1, hid1_t, gp1_t, x1, d1 = front(
        [x, xm, xp, d, dm, dp_, two_a, two_b], COLUMN, uk, dk
    )
    o_col, t_col = back_shares(column_kernel, 2, 256, hid1, gp1, uk, dk)
    hid2, gp2, hid2_t, gp2_t, x2, d2 = front([l1, l2, l3, l4, r1, r2, r3, r4], SIDE, uk, dk)

    up_away = packed(away, blocks[0], gp1_t, gp2_t, x1, x2)
    up_near = packed(near, blocks[0], gp1_t, gp2_t, x1, x2)
    side = back_shares(side_kernel, 8, 64, hid2, gp2, uk, dk)
    down_away = packed(away, blocks[1], hid1_t, hid2_t, d1, d2)
    down_near = packed(near, blocks[1], hid1_t, hid2_t, d1, d2)

    a1, a2, a3, a4 = (shift(v, dx=-1) for v in side[:4])
    b1, b2, b3, b4 = (shift(v, dx=1) for v in side[4:])
    za = shift(cat(add(o_col[192:224], a1[:32]), add(t_col[192:224], a1[32:])), dz=1)
    zb = shift(cat(add(o_col[224:256], b1[:32]), add(t_col[224:256], b1[32:])), dz=-1)

    def along_z(col, a, b, za, zb):
        p = cat(add(col[128:160], a[32:], za), add(col[160:192], b[32:]))
        m = cat(add(col[64:96], a[:32]), add(col[96:128], b[:32], zb))
        return shift(p, dz=1), shift(m, dz=-1)

    o_p, o_m = along_z(o_col, a2, b2, za[:32], zb[:32])
    t_p, t_m = along_z(t_col, a3, b3, za[32:], zb[32:])
    output = add(o_col[:64], cat(a4[:32], b4[:32]), o_p, o_m)
    grad_tokens = add(t_col[:64], cat(a4[32:], b4[32:]), t_p, t_m)

    grad_up = expand(True, own[0], *dp_sum(up_near, up_away))
    grad_down = expand(False, own[1], *dp_sum(down_near, down_away))
    return output, grad_tokens, grad_up, grad_down


def solution(mesh):
    placed = (
        P(("dp", "tensor"), None),
        P(None, "tensor"),
        P("tensor", None),
        P(None, "tensor"),
        P("tensor", None),
        P(("dp", "tensor"), None),
    )
    return jax.shard_map(
        local,
        mesh=mesh,
        in_specs=placed,
        out_specs=(
            P(("dp", "tensor"), None),
            P(("dp", "tensor"), None),
            P("dp", "tensor"),
            P("tensor", "dp"),
        ),
        check_vma=False,
    )
```

time: 611 us -> 298 us (0.49)
  waiting for transfers between devices: 381 us -> 117 us
  local copies, waits for them, and re-layouts: 140 us -> 29.4 us
  Pallas kernels: 0 us -> 91.1 us
  matrix products: 69.7 us -> 0 us
  starting transfers between devices: 0.64 us -> 44.4 us
  between operations: 14.1 us -> 1.43 us
  other arithmetic: 2.96 us -> 14.2 us
    reduce_scatter x4 -> x0, waiting for transfers between devices: 272 us -> none  [the longest x1 94.1 us: local(): lax.psum_scatter(jnp.dot(piece, down_kept, preferred_element_type=jnp.flo...]
    mul x8 -> x0, local copies, waits for them, and re-layouts: 138 us -> none  [apply_mask(): weight.reshape(nrows, B, ncols, B)]
    ppermute x0 -> x40, waiting for transfers between devices: none -> 117 us  [shift(): return lax.ppermute(value, AXES, pairs)]
    all_gather x2 -> x0, waiting for transfers between devices: 108 us -> none  [the longest x1 82.9 us: local(): lax.all_gather(cotangent, 'tensor', axis=0, tiled=True)]
    pallas_call x0 -> x11, Pallas kernels: none -> 91.1 us  [the longest x4 39.1 us: packed(): pl.pallas_call(packed_kernel, grid_spec=pltpu.PrefetchScalarGridSpec(num_...]
    dot_general x6 -> x0, matrix products: 69.7 us -> none  [the longest x1 12.9 us: local(): lax.dot_general(piece, up_kept, (((1,), (1,)), ((), ())), preferred_eleme...]
    ppermute x0 -> x40, starting transfers between devices: none -> 44.4 us  [shift(): return lax.ppermute(value, AXES, pairs)]
    unnamed x5 -> x84, local copies, waits for them, and re-layouts: 2.22 us -> 26.6 us
  transfers between devices with their start and end apart: 6 -> 40, of which waited for: 5 -> 16; matrix products, arithmetic and copies ran while one was open for 33% -> 6% of each run, Pallas kernels for 0% -> 22%
where the time goes in v1:
time: 298 us
  waiting for transfers between devices  117 us (39%)
  Pallas kernels  91.1 us (31%)
  starting transfers between devices  44.4 us (15%)
  local copies, waits for them, and re-layouts  29.4 us (10%)
  other arithmetic  14.2 us (5%)
    ppermute x40, waiting for transfers between devices, shift(): return lax.ppermute(value, AXES, pairs)  117 us
    ppermute x40, starting transfers between devices, shift(): return lax.ppermute(value, AXES, pairs)  44.4 us
    pallas_call x4, Pallas kernels, packed(): pl.pallas_call(packed_kernel, grid_spec=pltpu.PrefetchScalarGridSpec(num_...  39.1 us
    unnamed x84, local copies, waits for them, and re-layouts  26.6 us
    pallas_call x2, Pallas kernels, front(): pl.pallas_call(functools.partial(front_kernel, copies, n), grid=(F // til...  23.2 us
    pallas_call x2, Pallas kernels, back_shares(): pl.pallas_call(kernel, grid=(D // tile,), in_specs=[pl.BlockSpec((256, F)...  13.9 us
    pallas_call x1, Pallas kernels, kept_weights(): pl.pallas_call(mask_kernel, grid=(16,), in_specs=[pl.BlockSpec((64, 16),...  10.5 us
    convert_element_type x13, other arithmetic, add(): return total.astype(bf16)  9.48 us
  transfers between devices with their start and end apart: 40, of which 16 were waited for; matrix products, arithmetic and copies ran while one was open for 6% of the time, Pallas kernels for 22%

profile of v1, /device:TPU:24, one launch (start us, length us, event | category | flops | bytes accessed | tf_op | source)
XLA Modules:
  0.0 297.6 jit_solution(16830480188856643228)
XLA Ops:
  15.7 3.4 %copy-done.4 = bf16[4096,1024]{1,0:T(8,128)(2,1)S(1)} copy-done((bf16[4096,1024]{1,0:T(8,128)(2,1)S(1)}, bf16[4096,1024]{1,0:T(8,128)(2,1)}, u32[]{:S(2)}) %copy-start.4) | copy-done | bytes 8388632
  19.0 10.5 %kept_weights.1 = (bf16[4096,1024]{1,0:T(8,128)(2,1)S(1)}, bf16[1024,4096]{1,0:T(8,128)(2,1)S(1)}) custom-call(s32[64,16]{1,0:T(8,128)S(1)} %copy.36.mu, s32[16,64]{1,0:T(8,128)S(1)} %copy-done.17, bf16[4096,1024]{1,0:T(8,128)(2,1)S(1)} %copy-done.4, bf16[1024,4096]{1,0:T(8,128)(2,1)} %wd.1), custom_call_target="tpu_custom_call" | custom-call | bytes 37748736 | tf_op jit(solution)/shard_map/kept_weights/pallas_call | solution.py:64
  44.1 6.0 %collective-permute-done.6.refs_0_ = bf16[64,4096]{1,0:T(8,128)(2,1)S(1)} collective-permute-done((bf16[64,4096]{1,0:T(8,128)(2,1)S(1)}, bf16[64,4096]{1,0:T(8,128)(2,1)S(1)}, u32[]{:S(2)}, u32[]{:S(2)}) %collective-permute-start.6) | collective-permute-done | bytes 524320 | tf_op jit(solution)/shard_map/ppermute | solution.py:35
  56.4 11.2 %front.2 = (bf16[256,1024]{1,0:T(8,128)(2,1)S(1)}, bf16[256,1024]{1,0:T(8,128)(2,1)S(1)}, bf16[1024,256]{1,0:T(8,128)(2,1)S(1)}, bf16[1024,256]{1,0:T(8,128)(2,1...) custom-call(bf16[64,4096]{1,0:T(8,128)(2,1)S(1)} %copy-done.6, ...), custom_call_target="tpu_custom_call" | custom-call | flops 4294967296 | bytes 27262976 | tf_op jit(solution)/shard_map/front/pallas_call | solution.py:120
  70.8 4.9 %copy-done.2 = bf16[1024,4096]{1,0:T(8,128)(2,1)S(1)} copy-done((bf16[1024,4096]{1,0:T(8,128)(2,1)S(1)}, bf16[1024,4096]{1,0:T(8,128)(2,1)}, u32[]{:S(2)}) %copy-start.2) | copy-done | bytes 8388632
  77.8 6.6 %shares.2 = (bf16[256,4096]{1,0:T(8,128)(2,1)S(1)}, bf16[256,4096]{1,0:T(8,128)(2,1)S(1)}) custom-call(bf16[256,1024]{1,0:T(8,128)(2,1)S(1)} %copy-done.14, bf16[256,1024]{1,0:T(8,128)(2,1)S(1)} %copy-done.16, bf16[4096,1024]{1,0:T(8,128)(2,1)S(1)} %bitcast.25, bf16[1024,4096]{1,0:T(8,128)(2,1)S(1)} %copy-done.2), custom_call_target="tpu_custom_call" | custom-call | flops 4294967296 | bytes 23068672 | tf_op jit(solution)/shard_map/shares/pallas_call | solution.py:192
  87.2 12.1 %front.3 = (bf16[256,1024]{1,0:T(8,128)(2,1)S(1)}, bf16[256,1024]{1,0:T(8,128)(2,1)S(1)}, bf16[1024,256]{1,0:T(8,128)(2,1)S(1)}, bf16[1024,256]{1,0:T(8,128)(2,1...) custom-call(bf16[64,4096]{1,0:T(8,128)(2,1)S(1)} %collective-permute-done.6.refs_0_, ...), custom_call_target="tpu_custom_call" | custom-call | flops 4294967296 | bytes 27262976 | tf_op jit(solution)/shard_map/front/pallas_call | solution.py:120
  99.3 10.3 %packed.7 = bf16[8,1280,128]{2,1,0:T(8,128)(2,1)} custom-call(s32[8]{0:T(128)S(1)} %broadcast_xor_fusion.groups, s32[16,40]{1,0:T(8,128)S(1)} %get-tuple-element.100.blocks, bf16[1024,256]{1,0:T(8,128)(2,1)S(1)} %copy-done.30, bf16[1024,256]{1,0:T(8,128)(2,1)S(1)} %get-tuple-element.49.a2, bf16[256,4096]{1,0:T(8,128)(2,1)S(1)} %copy-done.21, ...), custom_call_target="tpu_custom_call" | custom-call | flops 2147483648 | bytes 6291456 | tf_op jit(solution)/shard_map/packed/pallas_call | solution.py:233
  109.8 3.4 %copy-done.3 = bf16[1024,4096]{1,0:T(8,128)(2,1)S(1)} copy-done((bf16[1024,4096]{1,0:T(8,128)(2,1)S(1)}, bf16[1024,4096]{1,0:T(8,128)(2,1)}, u32[]{:S(2)}) %copy-start.3) | copy-done | bytes 8388632
  113.2 7.3 %shares.3 = (bf16[64,4096]{1,0:T(8,128)(2,1)}, bf16[64,4096]{1,0:T(8,128)(2,1)S(1)}, bf16[64,4096]{1,0:T(8,128)(2,1)S(1)}, bf16[64,4096]{1,0:T(8,128)(2,1)S(1)},...) custom-call(bf16[256,1024]{1,0:T(8,128)(2,1)S(1)} %get-tuple-element, ...), custom_call_target="tpu_custom_call" | custom-call | flops 4294967296 | bytes 23068672 | tf_op jit(solution)/shard_map/shares/pallas_call | solution.py:192
  126.4 9.6 %packed.6 = bf16[8,1280,128]{2,1,0:T(8,128)(2,1)S(1)} custom-call(s32[8]{0:T(128)S(1)} %stack.39.groups, s32[16,40]{1,0:T(8,128)S(1)} %get-tuple-element.100.blocks, bf16[1024,256]{1,0:T(8,128)(2,1)S(1)} %copy-done.31, bf16[1024,256]{1,0:T(8,128)(2,1)S(1)} %copy-done.35, bf16[256,4096]{1,0:T(8,128)(2,1)S(1)} %copy-done.22, bf16[256,4096]{1,0:T(8,128)(2,1)S(1)} %copy-done.26), custom_call_target="tpu_custom_call" | custom-call | flops 2147483648 | bytes 6291456 | tf_op jit(solution)/shard_map/packed/pallas_call | solution.py:233
  136.0 9.6 %packed.4 = bf16[8,1280,128]{2,1,0:T(8,128)(2,1)S(1)} custom-call(s32[8]{0:T(128)S(1)} %stack.39.groups, s32[16,40]{1,0:T(8,128)S(1)} %get-tuple-element.101.blocks, bf16[1024,256]{1,0:T(8,128)(2,1)S(1)} %copy-done.28, bf16[1024,256]{1,0:T(8,128)(2,1)S(1)} %copy-done.33, bf16[256,4096]{1,0:T(8,128)(2,1)S(1)} %copy-done.19, bf16[256,4096]{1,0:T(8,128)(2,1)S(1)} %copy-done.24), custom_call_target="tpu_custom_call" | custom-call | flops 2147483648 | bytes 6291456 | tf_op jit(solution)/shard_map/packed/pallas_call | solution.py:233
  145.7 9.6 %packed.5 = bf16[8,1280,128]{2,1,0:T(8,128)(2,1)S(1)} custom-call(s32[8]{0:T(128)S(1)} %broadcast_xor_fusion.groups, s32[16,40]{1,0:T(8,128)S(1)} %get-tuple-element.101.blocks, bf16[1024,256]{1,0:T(8,128)(2,1)S(1)} %copy-done.28, bf16[1024,256]{1,0:T(8,128)(2,1)S(1)} %copy-done.33, bf16[256,4096]{1,0:T(8,128)(2,1)S(1)} %copy-done.19, ...), custom_call_target="tpu_custom_call" | custom-call | flops 2147483648 | bytes 6291456 | tf_op jit(solution)/shard_map/packed/pallas_call | solution.py:233
  159.5 21.2 %collective-permute-done.14 = bf16[64,4096]{1,0:T(8,128)(2,1)S(1)} collective-permute-done((bf16[64,4096]{1,0:T(8,128)(2,1)S(1)}, bf16[64,4096]{1,0:T(8,128)(2,1)S(1)}, u32[]{:S(2)}, u32[]{:S(2)}) %collective-permute-start.14) | collective-permute-done | bytes 524320 | tf_op jit(solution)/shard_map/ppermute | solution.py:35
  181.5 12.9 %collective-permute-done.18 = bf16[64,4096]{1,0:T(8,128)(2,1)S(1)} collective-permute-done((bf16[64,4096]{1,0:T(8,128)(2,1)S(1)}, bf16[64,4096]{1,0:T(8,128)(2,1)S(1)}, u32[]{:S(2)}, u32[]{:S(2)}) %collective-permute-start.18) | collective-permute-done | bytes 524320 | tf_op jit(solution)/shard_map/ppermute | solution.py:35
  195.4 12.5 %collective-permute-done.15 = bf16[64,4096]{1,0:T(8,128)(2,1)S(1)} collective-permute-done((bf16[64,4096]{1,0:T(8,128)(2,1)S(1)}, bf16[64,4096]{1,0:T(8,128)(2,1)S(1)}, u32[]{:S(2)}, u32[]{:S(2)}) %collective-permute-start.15) | collective-permute-done | bytes 524320 | tf_op jit(solution)/shard_map/ppermute | solution.py:35
  209.7 9.3 %collective-permute-done.22 = bf16[64,4096]{1,0:T(8,128)(2,1)S(1)} collective-permute-done((bf16[64,4096]{1,0:T(8,128)(2,1)S(1)}, bf16[64,4096]{1,0:T(8,128)(2,1)S(1)}, u32[]{:S(2)}, u32[]{:S(2)}) %collective-permute-start.22) | collective-permute-done | bytes 524320 | tf_op jit(solution)/shard_map/ppermute | solution.py:35
  226.5 8.9 %collective-permute-done.35 = bf16[1,1280,128]{2,1,0:T(8,128)(2,1)S(1)} collective-permute-done((bf16[1,1280,128]{2,1,0:T(8,128)(2,1)S(1)}, bf16[1,1280,128]{2,1,0:T(8,128)(2,1)S(1)}, u32[]{:S(2)}, u32[]{:S(2)}) %collective-permute-start.35) | collective-permute-done | bytes 327712 | tf_op jit(solution)/shard_map/ppermute | solution.py:35
  238.7 3.8 %collective-permute-done.29 = bf16[1,1280,128]{2,1,0:T(8,128)(2,1)S(1)} collective-permute-done((bf16[1,1280,128]{2,1,0:T(8,128)(2,1)S(1)}, bf16[1,1280,128]{2,1,0:T(8,128)(2,1)S(1)}, u32[]{:S(2)}, u32[]{:S(2)}) %collective-permute-start.29) | collective-permute-done | bytes 327712 | tf_op jit(solution)/shard_map/ppermute | solution.py:35
  243.7 8.7 %collective-permute-done.37 = bf16[1,1280,128]{2,1,0:T(8,128)(2,1)S(1)} collective-permute-done((bf16[1,1280,128]{2,1,0:T(8,128)(2,1)S(1)}, bf16[1,1280,128]{2,1,0:T(8,128)(2,1)S(1)}, u32[]{:S(2)}, u32[]{:S(2)}) %collective-permute-start.37) | collective-permute-done | bytes 327712 | tf_op jit(solution)/shard_map/ppermute | solution.py:35
  253.5 10.7 %collective-permute-done.31 = bf16[1,1280,128]{2,1,0:T(8,128)(2,1)S(1)} collective-permute-done((bf16[1,1280,128]{2,1,0:T(8,128)(2,1)S(1)}, bf16[1,1280,128]{2,1,0:T(8,128)(2,1)S(1)}, u32[]{:S(2)}, u32[]{:S(2)}) %collective-permute-start.31) | collective-permute-done | bytes 327712 | tf_op jit(solution)/shard_map/ppermute | solution.py:35
  270.1 9.1 %collective-permute-done.38 = bf16[2,1280,128]{2,1,0:T(8,128)(2,1)S(1)} collective-permute-done((bf16[2,1280,128]{2,1,0:T(8,128)(2,1)S(1)}, bf16[2,1280,128]{2,1,0:T(8,128)(2,1)S(1)}, u32[]{:S(2)}, u32[]{:S(2)}) %collective-permute-start.38) | collective-permute-done | bytes 655392 | tf_op jit(solution)/shard_map/ppermute | solution.py:35
  280.8 5.5 %collective-permute-done.32 = bf16[2,1280,128]{2,1,0:T(8,128)(2,1)S(1)} collective-permute-done((bf16[2,1280,128]{2,1,0:T(8,128)(2,1)S(1)}, bf16[2,1280,128]{2,1,0:T(8,128)(2,1)S(1)}, u32[]{:S(2)}, u32[]{:S(2)}) %collective-permute-start.32) | collective-permute-done | bytes 655392 | tf_op jit(solution)/shard_map/ppermute | solution.py:35
  291.4 3.9 %collective-permute-done.33.f = bf16[1,1280,128]{2,1,0:T(8,128)(2,1)S(1)} collective-permute-done((bf16[1,1280,128]{2,1,0:T(8,128)(2,1)S(1)}, bf16[1,1280,128]{2,1,0:T(8,128)(2,1)S(1)}, u32[]{:S(2)}, u32[]{:S(2)}) %collective-permute-start.33) | collective-permute-done | bytes 327712 | tf_op jit(solution)/shard_map/ppermute | solution.py:35
  (201 shorter events, 85.0 us)
Async XLA Ops:
  0.7 35.6 %collective-permute-start.2 = (bf16[64,4096]{1,0:T(8,128)(2,1)}, bf16[64,4096]{1,0:T(8,128)(2,1)S(1)}, u32[]{:S(2)}, u32[]{:S(2)}) collective-permute-start(bf16[64,4096]{1,0:T(8,128)(2,1)} %refs_3_.1), channel_id=1, source_target_pairs={{0,2},{8,10},{2,4},{10,12},{4,6},{12,14},{6,0},{14,8},{32,34},{40,... | collective-permute-start | bytes 1572872 | tf_op jit(solution)/shard_map/ppermute | solution.py:35
  2.6 33.8 %collective-permute-start.3 = (bf16[64,4096]{1,0:T(8,128)(2,1)}, bf16[64,4096]{1,0:T(8,128)(2,1)S(1)}, u32[]{:S(2)}, u32[]{:S(2)}) collective-permute-start(bf16[64,4096]{1,0:T(8,128)(2,1)} %refs_3_.1), channel_id=1, source_target_pairs={{0,6},{8,14},{2,0},{10,8},{4,2},{12,10},{6,4},{14,12},{32,38},{40,... | collective-permute-start | bytes 1572872 | tf_op jit(solution)/shard_map/ppermute | solution.py:35
  4.8 31.6 %collective-permute-start = (bf16[64,4096]{1,0:T(8,128)(2,1)}, bf16[64,4096]{1,0:T(8,128)(2,1)S(1)}, u32[]{:S(2)}, u32[]{:S(2)}) collective-permute-start(bf16[64,4096]{1,0:T(8,128)(2,1)} %refs_0_.1), channel_id=1, source_target_pairs={{0,2},{8,10},{2,4},{10,12},{4,6},{12,14},{6,0},{14,8},{32,34},{40,... | collective-permute-start | bytes 1572872 | tf_op jit(solution)/shard_map/ppermute | solution.py:35
  4.8 31.7 %collective-permute-start.1 = (bf16[64,4096]{1,0:T(8,128)(2,1)}, bf16[64,4096]{1,0:T(8,128)(2,1)S(1)}, u32[]{:S(2)}, u32[]{:S(2)}) collective-permute-start(bf16[64,4096]{1,0:T(8,128)(2,1)} %refs_0_.1), channel_id=1, source_target_pairs={{0,6},{8,14},{2,0},{10,8},{4,2},{12,10},{6,4},{14,12},{32,38},{40,... | collective-permute-start | bytes 1572872 | tf_op jit(solution)/shard_map/ppermute | solution.py:35
  11.0 32.9 %collective-permute-start.10 = (bf16[64,4096]{1,0:T(8,128)(2,1)}, bf16[64,4096]{1,0:T(8,128)(2,1)S(1)}, u32[]{:S(2)}, u32[]{:S(2)}) collective-permute-start(bf16[64,4096]{1,0:T(8,128)(2,1)} %pad_maximum_fusion.10), channel_id=1, source_target_pairs={{0,17},{8,25},{2,19},{10,27},{4,21},{12,29},{6,23},{14,31},{32,49}... | collective-permute-start | bytes 1572872 | tf_op jit(solution)/shard_map/ppermute | solution.py:35
  44.0 43.2 %collective-permute-start.12 = (bf16[64,4096]{1,0:T(8,128)(2,1)}, bf16[64,4096]{1,0:T(8,128)(2,1)}, u32[]{:S(2)}, u32[]{:S(2)}) collective-permute-start(bf16[64,4096]{1,0:T(8,128)(2,1)} %get-tuple-element.96), channel_id=1, source_target_pairs={{0,17},{8,25},{2,19},{10,27},{4,21},{12,29},{6,23},{14,31},{32,49}... | collective-permute-start | bytes 1572872 | tf_op jit(solution)/shard_map/ppermute | solution.py:35
  50.1 37.1 %collective-permute-start.7 = (bf16[64,4096]{1,0:T(8,128)(2,1)}, bf16[64,4096]{1,0:T(8,128)(2,1)}, u32[]{:S(2)}, u32[]{:S(2)}) collective-permute-start(bf16[64,4096]{1,0:T(8,128)(2,1)} %get-tuple-element.99), channel_id=1, source_target_pairs={{0,1},{8,9},{2,3},{10,11},{4,5},{12,13},{6,7},{14,15},{32,33},{40,... | collective-permute-start | bytes 1572872 | tf_op jit(solution)/shard_map/ppermute | solution.py:35
  50.2 37.0 %collective-permute-start.8 = (bf16[64,4096]{1,0:T(8,128)(2,1)}, bf16[64,4096]{1,0:T(8,128)(2,1)}, u32[]{:S(2)}, u32[]{:S(2)}) collective-permute-start(bf16[64,4096]{1,0:T(8,128)(2,1)} %get-tuple-element.98), channel_id=1, source_target_pairs={{0,1},{8,9},{2,3},{10,11},{4,5},{12,13},{6,7},{14,15},{32,33},{40,... | collective-permute-start | bytes 1572872 | tf_op jit(solution)/shard_map/ppermute | solution.py:35
  52.7 34.4 %collective-permute-start.13 = (bf16[64,4096]{1,0:T(8,128)(2,1)}, bf16[64,4096]{1,0:T(8,128)(2,1)}, u32[]{:S(2)}, u32[]{:S(2)}) collective-permute-start(bf16[64,4096]{1,0:T(8,128)(2,1)} %collective-permute-done.5.refs_7_), channel_id=1, source_target_pairs={{0,17},{8,25},{2,19},{10,27},{4,21},{12,29},{6,23},{14,31},{32,49}... | collective-permute-start | bytes 1572872 | tf_op jit(solution)/shard_map/ppermute | solution.py:35
  56.3 30.9 %collective-permute-start.9 = (bf16[64,4096]{1,0:T(8,128)(2,1)}, bf16[64,4096]{1,0:T(8,128)(2,1)}, u32[]{:S(2)}, u32[]{:S(2)}) collective-permute-start(bf16[64,4096]{1,0:T(8,128)(2,1)} %collective-permute-done.4.refs_6_), channel_id=1, source_target_pairs={{0,1},{8,9},{2,3},{10,11},{4,5},{12,13},{6,7},{14,15},{32,33},{40,... | collective-permute-start | bytes 1572872 | tf_op jit(solution)/shard_map/ppermute | solution.py:35
  109.7 113.9 %collective-permute-start.34 = (bf16[8,1280,128]{2,1,0:T(8,128)(2,1)}, bf16[8,1280,128]{2,1,0:T(8,128)(2,1)}, u32[]{:S(2)}, u32[]{:S(2)}) collective-permute-start(bf16[8,1280,128]{2,1,0:T(8,128)(2,1)} %packed.7), channel_id=1, source_target_pairs={{0,8},{8,0},{2,10},{10,2},{4,12},{12,4},{6,14},{14,6},{32,40},{40,... | collective-permute-start | bytes 7864328 | tf_op jit(solution)/shard_map/ppermute | solution.py:35
  120.5 34.8 %collective-permute-start.21 = (bf16[64,4096]{1,0:T(8,128)(2,1)}, bf16[64,4096]{1,0:T(8,128)(2,1)S(1)}, u32[]{:S(2)}, u32[]{:S(2)}) collective-permute-start(bf16[64,4096]{1,0:T(8,128)(2,1)} %get-tuple-element.41), channel_id=1, source_target_pairs={{0,1},{8,9},{2,3},{10,11},{4,5},{12,13},{6,7},{14,15},{32,33},{40,... | collective-permute-start | bytes 1572872 | tf_op jit(solution)/shard_map/ppermute | solution.py:35
  122.3 36.2 %collective-permute-start.17 = (bf16[64,4096]{1,0:T(8,128)(2,1)}, bf16[64,4096]{1,0:T(8,128)(2,1)S(1)}, u32[]{:S(2)}, u32[]{:S(2)}) collective-permute-start(bf16[64,4096]{1,0:T(8,128)(2,1)} %get-tuple-element.38), channel_id=1, source_target_pairs={{0,17},{8,25},{2,19},{10,27},{4,21},{12,29},{6,23},{14,31},{32,49}... | collective-permute-start | bytes 1572872 | tf_op jit(solution)/shard_map/ppermute | solution.py:35
  124.2 56.6 %collective-permute-start.16 = (bf16[64,4096]{1,0:T(8,128)(2,1)S(1)}, bf16[64,4096]{1,0:T(8,128)(2,1)S(1)}, u32[]{:S(2)}, u32[]{:S(2)}) collective-permute-start(bf16[64,4096]{1,0:T(8,128)(2,1)S(1)} %get-tuple-element.37), channel_id=1, source_target_pairs={{0,17},{8,25},{2,19},{10,27},{4,21},{12,29},{6,23},{14,31},{32,49}... | collective-permute-start | bytes 1572872 | tf_op jit(solution)/shard_map/ppermute | solution.py:35
  126.3 83.3 %collective-permute-start.19 = (bf16[64,4096]{1,0:T(8,128)(2,1)S(1)}, bf16[64,4096]{1,0:T(8,128)(2,1)S(1)}, u32[]{:S(2)}, u32[]{:S(2)}) collective-permute-start(bf16[64,4096]{1,0:T(8,128)(2,1)S(1)} %get-tuple-element.40), channel_id=1, source_target_pairs={{0,1},{8,9},{2,3},{10,11},{4,5},{12,13},{6,7},{14,15},{32,33},{40,... | collective-permute-start | bytes 1572872 | tf_op jit(solution)/shard_map/ppermute | solution.py:35
  155.3 54.4 %collective-permute-start.24 = (bf16[64,4096]{1,0:T(8,128)(2,1)S(1)}, bf16[64,4096]{1,0:T(8,128)(2,1)S(1)}, u32[]{:S(2)}, u32[]{:S(2)}) collective-permute-start(bf16[64,4096]{1,0:T(8,128)(2,1)S(1)} %get-tuple-element.42), channel_id=1, source_target_pairs={{0,17},{8,25},{2,19},{10,27},{4,21},{12,29},{6,23},{14,31},{32,49}... | collective-permute-start | bytes 1572872 | tf_op jit(solution)/shard_map/ppermute | solution.py:35
  158.6 22.2 %collective-permute-start.14 = (bf16[64,4096]{1,0:T(8,128)(2,1)S(1)}, bf16[64,4096]{1,0:T(8,128)(2,1)S(1)}, u32[]{:S(2)}, u32[]{:S(2)}) collective-permute-start(bf16[64,4096]{1,0:T(8,128)(2,1)S(1)} %get-tuple-element.35), channel_id=1, source_target_pairs={{0,17},{8,25},{2,19},{10,27},{4,21},{12,29},{6,23},{14,31},{32,49}... | collective-permute-start | bytes 1572872 | tf_op jit(solution)/shard_map/ppermute | solution.py:35
  180.8 28.9 %collective-permute-start.25 = (bf16[64,4096]{1,0:T(8,128)(2,1)S(1)}, bf16[64,4096]{1,0:T(8,128)(2,1)S(1)}, u32[]{:S(2)}, u32[]{:S(2)}) collective-permute-start(bf16[64,4096]{1,0:T(8,128)(2,1)S(1)} %get-tuple-element.43), channel_id=1, source_target_pairs={{0,1},{8,9},{2,3},{10,11},{4,5},{12,13},{6,7},{14,15},{32,33},{40,... | collective-permute-start | bytes 1572872 | tf_op jit(solution)/shard_map/ppermute | solution.py:35
  219.7 44.8 %collective-permute-start.26 = (bf16[64,4096]{1,0:T(8,128)(2,1)S(1)}, bf16[64,4096]{1,0:T(8,128)(2,1)S(1)}, u32[]{:S(2)}, u32[]{:S(2)}) collective-permute-start(bf16[64,4096]{1,0:T(8,128)(2,1)S(1)} %pad_maximum_fusion.16), channel_id=1, source_target_pairs={{0,2},{8,10},{2,4},{10,12},{4,6},{12,14},{6,0},{14,8},{32,34},{40,... | collective-permute-start | bytes 1572872 | tf_op jit(solution)/shard_map/ppermute | solution.py:35
  220.6 46.0 %collective-permute-start.27 = (bf16[64,4096]{1,0:T(8,128)(2,1)S(1)}, bf16[64,4096]{1,0:T(8,128)(2,1)S(1)}, u32[]{:S(2)}, u32[]{:S(2)}) collective-permute-start(bf16[64,4096]{1,0:T(8,128)(2,1)S(1)} %pad_maximum_fusion.17), channel_id=1, source_target_pairs={{0,6},{8,14},{2,0},{10,8},{4,2},{12,10},{6,4},{14,12},{32,38},{40,... | collective-permute-start | bytes 1572872 | tf_op jit(solution)/shard_map/ppermute | solution.py:35
  223.5 63.2 %collective-permute-start.20 = (bf16[64,4096]{1,0:T(8,128)(2,1)S(1)}, bf16[64,4096]{1,0:T(8,128)(2,1)S(1)}, u32[]{:S(2)}, u32[]{:S(2)}) collective-permute-start(bf16[64,4096]{1,0:T(8,128)(2,1)S(1)} %pad_maximum_fusion.13), channel_id=1, source_target_pairs={{0,2},{8,10},{2,4},{10,12},{4,6},{12,14},{6,0},{14,8},{32,34},{40,... | collective-permute-start | bytes 1572872 | tf_op jit(solution)/shard_map/ppermute | solution.py:35
  237.2 30.6 %collective-permute-start.36 = (bf16[2,1280,128]{2,1,0:T(8,128)(2,1)S(1)}, bf16[2,1280,128]{2,1,0:T(8,128)(2,1)S(1)}, u32[]{:S(2)}, u32[]{:S(2)}) collective-permute-start(bf16[2,1280,128]{2,1,0:T(8,128)(2,1)S(1)} %pad_maximum_fusion.2), channel_id=1, source_target_pairs={{0,32},{8,40},{2,34},{10,42},{4,36},{12,44},{6,38},{14,46},{32,64}... | collective-permute-start | bytes 1966088 | tf_op jit(solution)/shard_map/ppermute | solution.py:35
  266.6 19.7 %collective-permute-start.32 = (bf16[2,1280,128]{2,1,0:T(8,128)(2,1)S(1)}, bf16[2,1280,128]{2,1,0:T(8,128)(2,1)S(1)}, u32[]{:S(2)}, u32[]{:S(2)}) collective-permute-start(bf16[2,1280,128]{2,1,0:T(8,128)(2,1)S(1)} %pad_maximum_fusion.1), channel_id=1, source_target_pairs={{0,96},{8,104},{2,98},{10,106},{4,100},{12,108},{6,102},{14,110},{... | collective-permute-start | bytes 1966088 | tf_op jit(solution)/shard_map/ppermute | solution.py:35
  267.8 19.0 %collective-permute-start.23 = (bf16[64,4096]{1,0:T(8,128)(2,1)S(1)}, bf16[64,4096]{1,0:T(8,128)(2,1)S(1)}, u32[]{:S(2)}, u32[]{:S(2)}) collective-permute-start(bf16[64,4096]{1,0:T(8,128)(2,1)S(1)} %pad_maximum_fusion.15), channel_id=1, source_target_pairs={{0,6},{8,14},{2,0},{10,8},{4,2},{12,10},{6,4},{14,12},{32,38},{40,... | collective-permute-start | bytes 1572872 | tf_op jit(solution)/shard_map/ppermute | solution.py:35
  (57 other events, 634.3 us)
